TPU v7x, 32 devices: a whole 2x2x4 slice. The times are simulated.
32 devices in a mesh: dp: 2 (over x), segment: 4 (over y, core), seq: 4 (over z).
Axes of the slice: x: 2, y: 2, z: 4, core: 2. Of those that a mesh axis runs over, the one named last changes fastest.
Arguments:
- layer_inputs: bfloat16 [4, 2, 512, 1024], P('segment', 'dp', 'seq'), may hold values from -24 to 24
- ln_gain: float32 [4, 1024], P('segment'), may hold values from 1 to 4
- ln_bias: float32 [4, 1024], P('segment'), may hold values from -3 to 3
- qkv_weight: bfloat16 [4, 1024, 3072], P('segment', 'dp'), may hold values from -0.1875 to 0.1875
- out_weight: bfloat16 [4, 1024, 1024], P('segment', 'dp'), may hold values from -0.1875 to 0.1875
- dec_embed: bfloat16 [1024, 512], replicated, may hold values from -0.1875 to 0.1875
- decoder_grad: bfloat16 [2, 2048, 512], P('dp', 'seq'), may hold values from -6 to 6
- previous: bfloat16 [4, 2, 512, 1024], P('segment', 'dp', 'seq'), may hold values from -6 to 6
- visible: int32 [2, 512], P('dp'), may hold values from 0 to 2047, as said below
Outputs:
- layer_grads: bfloat16 [4, 2, 512, 1024], P('segment', 'dp', 'seq')
Inputs may be any that keep to these rules, and one draw needn't show every extreme that they name: `visible`: each row lists 512 distinct patch ids of one crop in ascending order. Of one crop's ids, at most 240 and at least 16 lie in any block of 512 consecutive patches (one device's block of decoder_grad), and in every crop some block holds exactly 240 and some exactly 16.
All inputs are finite; a program needn't handle non-finite values.
Results may differ from a plain program's by a relative error of at most 0.0055.
The roundings to bfloat16 on the way count: a program that leaves them out, or rounds other values in their place, can miss the bound.
Values may be sent and summed in bfloat16 or wider, within the bound.
A program may use at most 64 MiB of HBM per device.

v0:
```python
import jax
import jax.numpy as jnp
from jax import lax
from jax.sharding import PartitionSpec as P

HEADS = 16


eps_norm = 1e-06


def shifted(block, axis, distance):
    devices = range(lax.axis_size(axis))
    route = [(i - distance, i) for i in devices if i - distance in devices]
    return lax.ppermute(block, axis, route)


def contract_last(left_side, right_side):
    return lax.dot_general(
        left_side, right_side, (((1,), (1,)), ((), ())), preferred_element_type=jnp.float32
    )


def contract_first(left_side, right_side):
    return lax.dot_general(
        left_side, right_side, (((0,), (0,)), ((), ())), preferred_element_type=jnp.float32
    )


def block_backward(query_rows, key_rows, value_rows, grad_out, scaling):
    visible_rows = key_rows.shape[0]
    head_size = key_rows.shape[1]
    block_rows = min(512, visible_rows)
    block_count = visible_rows // block_rows
    query_blocks = query_rows.reshape(block_count, block_rows, head_size)
    grad_blocks = grad_out.reshape(block_count, block_rows, head_size)

    def block_step(running, pieces):
        key_grad, value_grad = running
        query_block, grad_block = pieces
        scores = contract_last(query_block, key_rows) * scaling
        row_top = jnp.max(scores, axis=1, keepdims=True)
        weights = jnp.exp(scores - row_top)
        probability = weights / jnp.sum(weights, axis=1, keepdims=True)
        prob_low = probability.astype(jnp.bfloat16)
        output = jnp.dot(prob_low, value_rows, preferred_element_type=jnp.float32)
        row_delta = jnp.sum(grad_block.astype(jnp.float32) * output, axis=1, keepdims=True)
        grad_probs = contract_last(grad_block, value_rows)
        grad_scores = (probability * (grad_probs - row_delta)).astype(jnp.bfloat16)
        query_grad = (
            jnp.dot(grad_scores, key_rows, preferred_element_type=jnp.float32) * scaling
        ).astype(jnp.bfloat16)
        key_grad = key_grad + contract_first(grad_scores, query_block) * scaling
        value_grad = value_grad + contract_first(prob_low, grad_block)
        return ((key_grad, value_grad), query_grad)

    start_state = (
        jnp.zeros((visible_rows, head_size), jnp.float32),
        jnp.zeros((visible_rows, head_size), jnp.float32),
    )
    (key_grad, value_grad), query_grads = lax.scan(
        block_step, start_state, (query_blocks, grad_blocks)
    )
    return (
        query_grads.reshape(visible_rows, head_size),
        key_grad.astype(jnp.bfloat16),
        value_grad.astype(jnp.bfloat16),
    )


def on_device(
    layer_inputs,
    ln_gain,
    ln_bias,
    qkv_weight,
    out_weight,
    dec_embed,
    decoder_grad,
    previous,
    visible,
):
    qkv_full, out_full = (
        lax.all_gather(qkv_weight[0], "dp", axis=0, tiled=True),
        lax.all_gather(out_weight[0], "dp", axis=0, tiled=True),
    )
    tokens = layer_inputs[0, 0]
    tok_dev = tokens.shape[0]
    width = tokens.shape[1]
    groups = lax.axis_size("seq")
    seq_rank = lax.axis_index("seq")
    segment_rank = lax.axis_index("segment")
    segments = lax.axis_size("segment")
    patch_grid = decoder_grad[0]
    patch_dev = patch_grid.shape[0]
    patch_ids = visible[0]
    capacity = 15 * tok_dev // 8
    bounds = jnp.arange(groups + 1, dtype=jnp.int32) * patch_dev
    starts = jnp.sum((patch_ids[None, :] < bounds[:, None]).astype(jnp.int32), axis=1)
    region_begin = starts[seq_rank]
    region_finish = starts[seq_rank + 1]
    padded = jnp.concatenate([patch_ids, jnp.zeros((capacity,), jnp.int32)])
    picked = lax.dynamic_slice_in_dim(padded, region_begin, capacity)
    alive_slot = jnp.arange(capacity, dtype=jnp.int32) < region_finish - region_begin
    local_ids = jnp.clip(picked - seq_rank * patch_dev, 0, patch_dev - 1)
    region_rows = jnp.where(
        alive_slot[:, None], jnp.take(patch_grid, local_ids, axis=0), jnp.zeros((), jnp.bfloat16)
    )
    wide_rows = contract_last(region_rows, dec_embed).astype(jnp.bfloat16)
    arrived = lax.all_gather(wide_rows, "seq", axis=0, tiled=True)
    own_ids = lax.dynamic_slice_in_dim(patch_ids, seq_rank * tok_dev, tok_dev)
    owner_ids = own_ids // patch_dev
    global_rank = seq_rank * tok_dev + jnp.arange(tok_dev, dtype=jnp.int32)
    slot_ids = owner_ids * capacity + (global_rank - jnp.take(starts, owner_ids))
    fetched = jnp.take(arrived, slot_ids, axis=0)
    incoming = shifted(previous[0, 0], "segment", -1)
    cotangent = incoming + jnp.where(segment_rank == segments - 1, fetched, jnp.zeros_like(fetched))
    norm_gain = ln_gain[0]
    norm_bias = ln_bias[0]
    values = tokens.astype(jnp.float32)
    center = values - jnp.mean(values, axis=1, keepdims=True)
    spread = jnp.sqrt(jnp.mean(center * center, axis=1, keepdims=True) + eps_norm)
    normed = center / spread
    lowered = (normed * norm_gain + norm_bias).astype(jnp.bfloat16)
    projected = jnp.dot(lowered, qkv_full, preferred_element_type=jnp.float32).astype(jnp.bfloat16)
    grad_attn = contract_last(cotangent, out_full).astype(jnp.bfloat16)
    head_count = HEADS // groups
    head_size = width // HEADS
    packed = jnp.concatenate(
        [
            projected.reshape(tok_dev, 3, groups, head_count, head_size),
            grad_attn.reshape(tok_dev, 1, groups, head_count, head_size),
        ],
        axis=1,
    )
    outgoing = packed.transpose(2, 3, 1, 0, 4).reshape(groups, -1)
    received = lax.all_to_all(outgoing, "seq", split_axis=0, concat_axis=0, tiled=True)
    head_data = (
        received.reshape(groups, head_count, 4, tok_dev, head_size)
        .transpose(1, 2, 0, 3, 4)
        .reshape(head_count, 4, groups * tok_dev, head_size)
    )
    scaling = head_size ** (-0.5)
    query_grad, key_grad, value_grad = jax.vmap(block_backward, in_axes=(0, 0, 0, 0, None))(
        head_data[:, 0], head_data[:, 1], head_data[:, 2], head_data[:, 3], scaling
    )
    back_data = jnp.stack([query_grad, key_grad, value_grad], axis=1)
    back_data = (
        back_data.reshape(head_count, 3, groups, tok_dev, head_size)
        .transpose(2, 0, 1, 3, 4)
        .reshape(groups, -1)
    )
    gathered = lax.all_to_all(back_data, "seq", split_axis=0, concat_axis=0, tiled=True)
    grad_proj = (
        gathered.reshape(groups, head_count, 3, tok_dev, head_size)
        .transpose(3, 2, 0, 1, 4)
        .reshape(tok_dev, 3 * width)
    )
    grad_norm = contract_last(grad_proj, qkv_full)
    scaled = grad_norm * norm_gain
    grad_in = (
        scaled
        - jnp.mean(scaled, axis=1, keepdims=True)
        - normed * jnp.mean(scaled * normed, axis=1, keepdims=True)
    ) / spread
    result = (cotangent.astype(jnp.float32) + grad_in).astype(jnp.bfloat16)
    return result[None, None]


def solution(mesh):
    placed = (
        P("segment", "dp", "seq", None),
        P("segment", None),
        P("segment", None),
        P("segment", "dp", None),
        P("segment", "dp", None),
        P(),
        P("dp", "seq", None),
        P("segment", "dp", "seq", None),
        P("dp", None),
    )
    return jax.shard_map(
        on_device,
        mesh=mesh,
        in_specs=placed,
        out_specs=P("segment", "dp", "seq", None),
        check_vma=False,
    )
```

profile of v0, /device:TPU:0, one launch (start us, length us, event | category | flops | bytes accessed | tf_op | source)
XLA Modules:
  0.0 317.3 jit_solution(4929110955753982767)
XLA Ops:
  6.5 1.0 convert_reduce_fusion.1
  7.5 0.7 fusion.50
  11.5 0.8 compare_and_fusion
  12.3 2.3 gather_fusion
  14.6 1.3 convolution_convert_fusion
  16.0 0.7 all-gather.10.cloned.1.call-update
  16.7 0.7 all-gather.8.cloned.1.call-update
  17.4 1.3 collective-permute-start
  18.7 3.8 %compare_and_fusion.1 = (pred[128]{0:T(512)(128)(4,1)S(1)}, s32[128,1]{0,1:T(1,128)S(1)}, s32[128,1]{0,1:T(1,128)S(1)}) fusion(s32[]{:T(128)S(6)} %mul.83, s32[1,512]{1,0:T(1,128)} %param.17, s32[]{:T(128)S(6)} %select_n.114, s32[]{:T(128)} %bitcast.8, s32[]{:T(128)} %bitcast.7, s32[]{:T(128)} %bitcast.6, s32[]{:T(128)} %bitcast.5, s32[]{:T(128)} %bitcast.4), kind=kLoop, calls=%fused_computation.69 | loop fusion | flops 7424 | bytes 1692 | tf_op jit(solution)/shard_map/jit(_take)/and | solution.py:114
  23.0 39.4 %all-gather.6.cloned.1.call-done = bf16[960,1024]{1,0:T(8,128)(2,1)} async-done(((bf16[240,1024]{1,0:T(8,128)(2,1)}), bf16[960,1024]{1,0:T(8,128)(2,1)}) %all-gather.6.cloned.1.call-update) | async-done | bytes 1966096 | tf_op jit(solution)/shard_map/all_gather | solution.py:109
  62.3 2.8 gather_fusion.1
  65.2 30.6 %all-gather.10.cloned.1.call-done = bf16[1,1024,1024]{2,1,0:T(8,128)(2,1)} async-done(((bf16[1,512,1024]{2,1,0:T(8,128)(2,1)}), bf16[1,1024,1024]{2,1,0:T(8,128)(2,1)}) %all-gather.10.cloned.1.call-update) | async-done | bytes 2097168 | tf_op jit(solution)/shard_map/all_gather | solution.py:84
  95.8 2.4 fusion.18
  98.5 79.3 %all-gather.8.cloned.1.call-done = bf16[1,1024,3072]{2,1,0:T(8,128)(2,1)} async-done(((bf16[1,512,3072]{2,1,0:T(8,128)(2,1)}), bf16[1,1024,3072]{2,1,0:T(8,128)(2,1)}) %all-gather.8.cloned.1.call-update) | async-done | bytes 6291472 | tf_op jit(solution)/shard_map/all_gather | solution.py:83
  177.8 4.8 %fusion.6 = bf16[128,3072]{1,0:T(8,128)(2,1)} fusion(bf16[1,1024,3072]{2,1,0:T(8,128)(2,1)} %all-gather.8.cloned.1.call-done, f32[1024]{0:T(1024)S(1)} %bitcast.142, f32[1024]{0:T(1024)S(1)} %bitcast.143, bf16[1,1,128,1024]{3,2,1,0:T(8,128)(2,1)S(1)} %copy-done.2, f32[128]{0:T(128)S(1)} %add_sqrt_fusion, f32[128]{0:T(128)S(1)} %broadcast_multiply_fusion.2), kind=kOutput, calls=%fused_computation.11 | convolution fusion | flops 806486016 | bytes 7349248 | tf_op jit(solution)/shard_map/dot_general | solution.py:124
  182.6 1.5 copy.44
  184.2 2.3 copy.46
  186.5 3.0 all_to_all.16
  189.5 0.5 broadcast.388
  190.1 8.4 %reduce.3 = bf16[4,131072]{1,0:T(4,128)(2,1)} reduce(bf16[4,1,131072]{2,1,0:T(2,128)(2,1)S(1)} %all_to_all.16, bf16[]{:T(256)} %broadcast.388), dimensions={1}, to_apply=%all_to_all.16.reduce_sub_computation | reduce | bytes 2097154 | tf_op jit(solution)/shard_map/all_to_all | solution.py:136
  198.5 2.3 reshape.285
  200.8 30.4 %all_to_all.20 = bf16[4,2,65536]{2,1,0:T(2,128)(2,1)} all-to-all(bf16[4,2,65536]{2,1,0:T(2,128)(2,1)S(1)} %reshape.285), channel_id=1, replica_groups=mesh['dp'=2,'segment'=4,'seq'=4] {'seq'}, dimensions={0} | all-to-all | bytes 2097152 | tf_op jit(solution)/shard_map/all_to_all | solution.py:136
  231.2 2.6 reshape.286
  233.8 7.8 %reduce.1 = bf16[4,131072]{1,0:T(4,128)(2,1)} reduce(bf16[4,1,131072]{2,1,0:T(2,128)(2,1)S(1)} %reshape.286, bf16[]{:T(256)} %constant.131), dimensions={1}, to_apply=%all_to_all.13.reduce_sub_computation | reduce | bytes 2097154 | tf_op jit(solution)/shard_map/all_to_all | solution.py:136
  241.6 3.0 reshape.228
  244.6 2.2 copy.48
  246.8 1.7 reshape.229
  248.5 3.5 %fusion.51 = (f32[4,512]{1,0:T(4,128)S(1)}, f32[4,512,512]{1,2,0:T(8,128)}) fusion(bf16[4,4,512,64]{2,3,0,1:T(8,128)(2,1)S(1)} %reshape.229), kind=kOutput, calls=%fused_computation.98 | convolution fusion | flops 137363968 | bytes 4726784 | tf_op jit(solution)/shard_map/vmap()/while/body/eval_jaxpr/sub | solution.py:43
  252.0 2.8 fusion.14
  254.8 0.7 convolution_convert_fusion.1
  255.6 0.5 fusion.23
  256.1 0.9 copy-done.1
  257.0 0.8 multiply_convert_fusion
  257.8 0.8 fusion.21
  258.5 0.5 fusion.22
  259.5 1.1 copy.55
  260.6 1.1 copy.54
  261.7 1.5 maximum_bitcast_fusion
  263.3 2.2 all_to_all.17
  265.4 6.9 %reduce.4 = bf16[4,98304]{1,0:T(4,128)(2,1)S(1)} reduce(bf16[4,1,98304]{2,1,0:T(2,128)(2,1)} %all_to_all.17, bf16[]{:T(256)} %broadcast.388), dimensions={1}, to_apply=%all_to_all.17.reduce_sub_computation | reduce | bytes 1572866 | tf_op jit(solution)/shard_map/all_to_all | solution.py:152
  272.4 0.8 reshape.287
  273.2 22.4 %all_to_all.21 = bf16[4,2,49152]{2,1,0:T(2,128)(2,1)S(1)} all-to-all(bf16[4,2,49152]{2,1,0:T(2,128)(2,1)S(1)} %reshape.287), channel_id=1, replica_groups=mesh['dp'=2,'segment'=4,'seq'=4] {'seq'}, dimensions={0} | all-to-all | bytes 1572864 | tf_op jit(solution)/shard_map/all_to_all | solution.py:152
  295.6 0.7 reshape.288
  296.3 5.1 %reduce.2 = bf16[4,98304]{1,0:T(4,128)(2,1)S(1)} reduce(bf16[4,1,98304]{2,1,0:T(2,128)(2,1)S(1)} %reshape.288, bf16[]{:T(256)} %constant.131), dimensions={1}, to_apply=%all_to_all.15.reduce_sub_computation | reduce | bytes 1572866 | tf_op jit(solution)/shard_map/all_to_all | solution.py:152
  301.4 1.2 reshape.230
  302.6 1.4 copy.58
  304.1 5.4 %fusion.49 = (f32[128]{0:T(128)S(1)}, f32[128]{0:T(128)S(1)}, f32[128,1024]{1,0:T(8,128)S(1)}) fusion(f32[128]{0:T(128)S(1)} %add_sqrt_fusion, f32[128]{0:T(128)S(1)} %broadcast_multiply_fusion.2, bf16[1,1,128,1024]{3,2,1,0:T(8,128)(2,1)S(1)} %copy-done.3, f32[1024]{0:T(1024)S(1)} %bitcast.144, bf16[128,3072]{0,1:T(8,128)(2,1)} %bitcast.138, ...), kind=kOutput, calls=%fused_computation.96 | convolution fusion | flops 806223616 | bytes 7870464 | tf_op jit(solution)/shard_map/dot_general | solution.py:19
  309.5 1.0 fusion.32
  (42 shorter events, 1.3 us)
Async XLA Ops:
  6.5 8.0 %copy-start = (bf16[1024,512]{1,0:T(8,128)(2,1)S(1)}, bf16[1024,512]{1,0:T(8,128)(2,1)}, u32[]{:S(2)}) copy-start(bf16[1024,512]{1,0:T(8,128)(2,1)} %param.14) | copy-start | bytes 3145732
  6.5 55.8 %all-gather.6.cloned.1.call-start = ((), (), s32[]{:S(2)}) async-start(), calls=%async_computation.2 | async-start | bytes 2457600 | tf_op jit(solution)/shard_map/all_gather | solution.py:109
  15.9 1.5 copy-start.8
  15.9 6.6 %copy-start.2 = (bf16[1,1,128,1024]{3,2,1,0:T(8,128)(2,1)S(1)}, bf16[1,1,128,1024]{3,2,1,0:T(8,128)(2,1)}, u32[]{:S(2)}) copy-start(bf16[1,1,128,1024]{3,2,1,0:T(8,128)(2,1)} %param.9) | copy-start | bytes 786436
  15.9 79.9 %all-gather.10.cloned.1.call-start = ((), (), s32[]{:S(2)}) async-start(), calls=%async_computation.4 | async-start | bytes 3145728 | tf_op jit(solution)/shard_map/all_gather | solution.py:84
  16.7 161.1 %all-gather.8.cloned.1.call-start = ((), (), s32[]{:S(2)}) async-start(), calls=%async_computation.3 | async-start | bytes 9437184 | tf_op jit(solution)/shard_map/all_gather | solution.py:83
  17.4 47.8 %collective-permute-start = (bf16[128,1024]{1,0:T(8,128)(2,1)S(1)}, bf16[128,1024]{1,0:T(8,128)(2,1)S(1)}, u32[]{:S(2)}, u32[]{:S(2)}) collective-permute-start(bf16[128,1024]{1,0:T(8,128)(2,1)S(1)} %bitcast.141), channel_id=1, source_target_pairs={{4,0},{8,4},{12,8},{5,1},{9,5},{13,9},{6,2},{10,6},{14,10},{7,3},{... | collective-permute-start | bytes 786440 | tf_op jit(solution)/shard_map/ppermute | solution.py:15
  65.2 117.4 %copy-start.4 = (bf16[128,1024]{1,0:T(8,128)(2,1)}, bf16[128,1024]{1,0:T(8,128)(2,1)S(1)}, u32[]{:S(2)}) copy-start(bf16[128,1024]{1,0:T(8,128)(2,1)S(1)} %gather_fusion.1) | copy-start | bytes 786436
  65.2 112.6 %copy-start.9 = (f32[1,1024]{1,0:T(1,128)S(1)}, f32[1,1024]{1,0:T(1,128)}, u32[]{:S(2)}) copy-start(f32[1,1024]{1,0:T(1,128)} %param.11) | copy-start | bytes 12292
  65.2 112.6 %copy-start.10 = (f32[1,1024]{1,0:T(1,128)S(1)}, f32[1,1024]{1,0:T(1,128)}, u32[]{:S(2)}) copy-start(f32[1,1024]{1,0:T(1,128)} %param.10) | copy-start | bytes 12292
  65.2 117.4 %copy-start.6 = (bf16[128,1024]{1,0:T(8,128)(2,1)}, bf16[128,1024]{1,0:T(8,128)(2,1)S(1)}, u32[]{:S(2)}) copy-start(bf16[128,1024]{1,0:T(8,128)(2,1)S(1)} %collective-permute-done) | copy-start | bytes 786436
  254.8 2.2 copy-start.1
  302.6 1.4 copy-start.3
  304.0 5.4 %copy-start.5 = (bf16[128,1024]{1,0:T(8,128)(2,1)S(1)}, bf16[128,1024]{1,0:T(8,128)(2,1)}, u32[]{:S(2)}) copy-start(bf16[128,1024]{1,0:T(8,128)(2,1)} %copy-done.4) | copy-start | bytes 786436
  304.0 5.4 %copy-start.7 = (bf16[128,1024]{1,0:T(8,128)(2,1)S(1)}, bf16[128,1024]{1,0:T(8,128)(2,1)}, u32[]{:S(2)}) copy-start(bf16[128,1024]{1,0:T(8,128)(2,1)} %copy-done.6) | copy-start | bytes 786436
Sparse Core Ops, SparseCore 0:
  16.0 46.2 all-gather.5
  63.9 31.9 all-gather.9
  97.4 80.3 all-gather.7
where the time goes:
time: 322 us; the launch traced here: 317 us
  waiting for transfers between devices  151 us (47%)
  blocking collectives  52.8 us (16%)
  other arithmetic  39.6 us (12%)
  local copies, waits for them, and re-layouts  35.1 us (11%)
  matrix products  20.7 us (6%)
  between operations  17 us (5%)
    all_gather x1, waiting for transfers between devices, on_device(): lax.all_gather(qkv_weight[0], 'dp', axis=0, tiled=True)  79.3 us
    all_gather x1, waiting for transfers between devices, on_device(): arrived = lax.all_gather(wide_rows, 'seq', axis=0, tiled=True)  39.4 us
    all_gather x1, waiting for transfers between devices, on_device(): lax.all_gather(out_weight[0], 'dp', axis=0, tiled=True)  30.6 us
    all_to_all x1, blocking collectives, on_device(): lax.all_to_all(outgoing, 'seq', split_axis=0, concat_axis=0, tiled=True)  30.4 us
    all_to_all x1, blocking collectives, on_device(): lax.all_to_all(back_data, 'seq', split_axis=0, concat_axis=0, tiled=True)  22.4 us
    all_to_all x2, other arithmetic, on_device(): lax.all_to_all(outgoing, 'seq', split_axis=0, concat_axis=0, tiled=True)  16.2 us
    all_to_all x2, other arithmetic, on_device(): lax.all_to_all(back_data, 'seq', split_axis=0, concat_axis=0, tiled=True)  12 us
    dot_general x4, matrix products, contract_last(): lax.dot_general(left_side, right_side, (((1,), (1,)), ((), ())), preferre...  9.87 us
  transfers between devices with their start and end apart: 4, of which 3 were waited for; matrix products, arithmetic and copies ran while one was open for 3% of the time, Pallas kernels for 0%

commit v1 on v0

v1 whole, which is shorter than its diff:
```python
import functools

import jax
import jax.numpy as jnp
from jax import lax
from jax.experimental import pallas as pl
from jax.experimental.pallas import tpu as pltpu
from jax.sharding import PartitionSpec as P

HEADS = 16
EPS = 1e-06
MESH = pl.DeviceIdType.MESH
F32 = jnp.float32
BF16 = jnp.bfloat16


def contract_last(left_side, right_side):
    return lax.dot_general(
        left_side, right_side, (((1,), (1,)), ((), ())), preferred_element_type=F32
    )


def contract_first(left_side, right_side):
    return lax.dot_general(
        left_side, right_side, (((0,), (0,)), ((), ())), preferred_element_type=F32
    )


def head_backward(query_rows, key_rows, value_rows, grad_out, scaling):
    rows = query_rows.shape[0]
    step = min(512, rows)
    query_grads = []
    key_grad = value_grad = None
    for at in range(0, rows, step):
        query = query_rows[at : at + step]
        grad = grad_out[at : at + step]
        scores = contract_last(query, key_rows) * scaling
        weights = jnp.exp(scores - jnp.max(scores, axis=1, keepdims=True))
        probs = weights * (1.0 / jnp.sum(weights, axis=1, keepdims=True))
        probs_low = probs.astype(BF16)
        output = jnp.dot(probs_low, value_rows, preferred_element_type=F32)
        row_delta = jnp.sum(grad.astype(F32) * output, axis=1, keepdims=True)
        grad_probs = contract_last(grad, value_rows)
        grad_scores = (probs * (grad_probs - row_delta)).astype(BF16)
        query_grads.append(
            (jnp.dot(grad_scores, key_rows, preferred_element_type=F32) * scaling).astype(BF16)
        )
        key_part = contract_first(grad_scores, query) * scaling
        value_part = contract_first(probs_low, grad)
        key_grad = key_part if key_grad is None else key_grad + key_part
        value_grad = value_part if value_grad is None else value_grad + value_part
    query_grad = query_grads[0] if len(query_grads) == 1 else jnp.concatenate(query_grads, axis=0)
    return query_grad, key_grad.astype(BF16), value_grad.astype(BF16)


def kernel(
    dims,
    x_ref, gain_ref, bias_ref, prev_ref, ids_ref, w_ref, ow_ref, de_ref, dg_ref,
    out_ref,
    wg, wc, ow, de, dg, low, normed_ref, spread_ref, cot, go, ga, pk, pr,
    pj, gp, rb, gns, gnr,
    lw_sem, lo_sem, prev_s, prev_r, w_s, w_r, pk_s, pk_r, l_s, l_r, ct_s, ct_r,
    g_s, g_r, b_s, b_r, f_s, f_r, n_s, n_r,
):
    dp, segs, groups, tok, width, chunks, pair, head_size, sliced = dims
    cw = pair * head_size
    hw = chunks * cw
    depth = width // dp
    per_dp = groups // dp
    d = lax.axis_index("dp")
    s = lax.axis_index("segment")
    z = lax.axis_index("seq")
    last = s == segs - 1
    owner = z // per_dp

    def z_at(o):
        return lax.rem(z + o, groups)

    def d_at(o):
        return lax.rem(d + o, dp)

    def remote(src, dst, send, recv, dd, ss, zz):
        return pltpu.make_async_remote_copy(
            src_ref=src, dst_ref=dst, send_sem=send, recv_sem=recv,
            device_id=(dd, ss, zz), device_id_type=MESH,
        )

    def w_copies(o):
        g = z_at(o)
        if not sliced:
            return [pltpu.make_async_copy(w_ref.at[g], wg.at[g], lw_sem.at[o, 0, 0])]
        found = []
        for ch in range(chunks):
            for part in range(3):
                at = pl.multiple_of(part * width + g * hw + ch * cw, 128)
                found.append(
                    pltpu.make_async_copy(
                        w_ref.at[:, pl.ds(at, cw)],
                        wg.at[g, ch, :, pl.ds(part * cw, cw)],
                        lw_sem.at[o, ch, part],
                    )
                )
        return found

    local_w = [w_copies(o) for o in range(groups)]
    ow_copy = pltpu.make_async_copy(ow_ref, ow, lo_sem.at[0])
    de_copy = pltpu.make_async_copy(de_ref, de, lo_sem.at[1])
    dg_copy = pltpu.make_async_copy(dg_ref, dg, lo_sem.at[2])
    for copy in local_w[0]:
        copy.start()

    @pl.when(last)
    def _():
        dg_copy.start()
        de_copy.start()

    ow_copy.start()
    for o in range(1, groups):
        for copy in local_w[o]:
            copy.start()

    barrier = pltpu.get_barrier_semaphore()
    for od in range(dp):
        for oz in range(groups):
            if od or oz:
                pl.semaphore_signal(
                    barrier, inc=1, device_id=(d_at(od), s, z_at(oz)), device_id_type=MESH
                )

    pl.semaphore_signal(
        barrier, inc=1, device_id=(d, lax.rem(s + 1, segs), z), device_id_type=MESH
    )
    pl.semaphore_wait(barrier, dp * groups)

    down = jnp.maximum(s - 1, 0)
    prev_copy = remote(prev_ref, cot.at[d], prev_s.at[0], prev_r.at[0], d, down, z)

    @pl.when(s > 0)
    def _():
        prev_copy.start()

    def pick_copy(o):
        g = z_at(o)
        return remote(pk.at[g], pr.at[z], pk_s.at[g], pk_r.at[z], d, s, g)

    def arrive(dst, recv, dd, zz):
        remote(dst, dst, recv, recv, dd, s, zz).wait_recv()

    @pl.when(last)
    def _():
        dg_copy.wait()
        patches = dg.shape[0]
        patch_ids = lax.broadcasted_iota(jnp.int32, (patches, tok), 0) + z * patches
        for o in list(range(1, groups)) + [0]:
            g = z_at(o)
            hit = jnp.where(patch_ids == ids_ref[g], 1.0, 0.0).astype(BF16)
            rows = contract_first(hit, dg[...]).astype(BF16)
            if o:
                pk[g] = rows
                pick_copy(o).start()
            else:
                pr[z] = rows

    values = x_ref[...].astype(F32)
    center = values - jnp.mean(values, axis=1, keepdims=True)
    spread = jnp.sqrt(jnp.mean(center * center, axis=1, keepdims=True) + EPS)
    normed = center / spread
    normed_ref[...] = normed
    spread_ref[...] = jnp.broadcast_to(spread, spread_ref.shape)
    low[z] = (normed * gain_ref[...] + bias_ref[...]).astype(BF16)

    def low_copy(o):
        return remote(low.at[z], low.at[z], l_s.at[z_at(o)], l_r.at[z], d, s, z_at(o))

    for o in range(1, groups):
        low_copy(o).start()

    def w_copy(o, ch):
        dd = d_at(o)
        return remote(wg.at[z, ch], wc.at[d, ch], w_s.at[dd, ch], w_r.at[d, ch], dd, s, z)

    for copy in local_w[0]:
        copy.wait()
    for ch in range(chunks):
        for o in range(1, dp):
            w_copy(o, ch).start()

    @pl.when(s < segs - 1)
    def _():
        prev_copy.wait_recv()

    @pl.when(last)
    def _():
        for o in range(1, groups):
            arrive(pr.at[z_at(o)], pk_r.at[z_at(o)], d, z_at(o))
        picked = pr[0].astype(F32)
        for g in range(1, groups):
            picked = picked + pr[g].astype(F32)
        de_copy.wait()
        cot[d] = contract_last(picked.astype(BF16), de[...]).astype(BF16)

    def cot_copy(o):
        return remote(cot.at[d], cot.at[d], ct_s.at[d_at(o)], ct_r.at[d], d_at(o), s, z)

    for o in range(1, dp):
        cot_copy(o).start()

    def g_copy(c, j):
        g = d * per_dp + j
        return remote(go.at[c, j], ga.at[z], g_s.at[c, j], g_r.at[z], c, s, g)

    ow_copy.wait()
    for o in range(dp):
        c = d_at(o)
        if o:
            arrive(cot.at[c], ct_r.at[c], c, z)
        grads = contract_last(cot[c], ow[...]).astype(BF16)
        for j in range(per_dp):
            for ch in range(chunks):
                at = (j * chunks + ch) * cw
                go[c, j, ch] = grads[:, at : at + cw]
            if o:
                g_copy(c, j).start()
            else:
                mine = d * per_dp + j == z

                @pl.when(jnp.logical_not(mine))
                def _():
                    g_copy(c, j).start()

                @pl.when(mine)
                def _():
                    ga[z] = go[c, j]

    def back_copy(o, ch):
        g = z_at(o)
        return remote(gp.at[ch, g], rb.at[ch, d, z], b_s.at[ch, g], b_r.at[ch, z], d, s, g)

    def forward_copy(o, ch, g):
        dd = d_at(o)
        return remote(
            rb.at[ch, d, g], rb.at[ch, d, g], f_s.at[ch, dd, g], f_r.at[ch, d, g], dd, s, z
        )

    def forward(ch):
        for o in range(1, groups):
            g = z_at(o)
            arrive(rb.at[ch, d, g], b_r.at[ch, g], d, g)
            for od in range(1, dp):
                forward_copy(od, ch, g).start()

    scaling = head_size ** (-0.5)
    for ch in range(chunks):
        if ch == 0:
            for o in range(1, groups):
                arrive(low.at[z_at(o)], l_r.at[z_at(o)], d, z_at(o))
        total = None
        for o in range(dp):
            dd = d_at(o)
            if o:
                arrive(wc.at[dd, ch], w_r.at[dd, ch], dd, z)
            weights = wc[dd, ch] if o else wg[z, ch]
            columns = low[:, :, pl.ds(pl.multiple_of(dd * depth, depth), depth)]
            term = jnp.dot(
                columns.reshape(groups * tok, depth), weights, preferred_element_type=F32
            )
            total = term if total is None else total + term
        pj[...] = total.astype(BF16)
        if ch == 0:
            for src in range(groups):
                @pl.when(jnp.logical_not(jnp.logical_and(owner == d, src == z)))
                def _():
                    arrive(ga.at[src], g_r.at[src], owner, src)
        grad_rows = ga[:, ch].reshape(groups * tok, cw)
        found = ([], [], [])
        for h in range(pair):
            parts = [
                pj[:, part * cw + h * head_size : part * cw + (h + 1) * head_size]
                for part in range(3)
            ]
            result = head_backward(
                *parts, grad_rows[:, h * head_size : (h + 1) * head_size], scaling
            )
            for part in range(3):
                found[part].append(result[part])
        for part in range(3):
            whole = found[part][0] if pair == 1 else jnp.concatenate(found[part], axis=1)
            gp[ch, :, :, part * cw : (part + 1) * cw] = whole.reshape(groups, tok, cw)
        for o in range(1, groups):
            back_copy(o, ch).start()
        rb[ch, d, z] = gp[ch, z]
        for od in range(1, dp):
            forward_copy(od, ch, z).start()
        if ch:
            forward(ch - 1)
    forward(chunks - 1)
    for o in range(1, groups):
        for copy in local_w[o]:
            copy.wait()

    def half(c):
        def step(g, total):
            for ch in range(chunks):
                total = total + contract_last(rb[ch, c, g], wg[g, ch])
            return total

        return lax.fori_loop(0, groups, step, jnp.zeros((tok, depth), F32))

    def n_copy(o):
        c = d_at(o)
        return remote(gns.at[c], gnr.at[d], n_s.at[c], n_r.at[d], c, s, z)

    gnr[d] = half(d)
    for o in range(1, dp):
        c = d_at(o)
        for ch in range(chunks):
            for g in range(groups):
                arrive(rb.at[ch, c, g], f_r.at[ch, c, g], c, z)
        gns[c] = half(c)
        n_copy(o).start()
    for o in range(1, dp):
        arrive(gnr.at[d_at(o)], n_r.at[d_at(o)], d_at(o), z)
    grad_norm = jnp.concatenate([gnr[c] for c in range(dp)], axis=1)
    scaled = grad_norm * gain_ref[...]
    normed = normed_ref[...]
    grad_in = (
        scaled
        - jnp.mean(scaled, axis=1, keepdims=True)
        - normed * jnp.mean(scaled * normed, axis=1, keepdims=True)
    ) / spread_ref[:, :1]
    out_ref[...] = (cot[d].astype(F32) + grad_in).astype(BF16)

    @pl.when(s > 0)
    def _():
        prev_copy.wait_send()

    @pl.when(last)
    def _():
        for o in range(1, groups):
            pick_copy(o).wait_send()

    for o in range(1, groups):
        low_copy(o).wait_send()
        for ch in range(chunks):
            back_copy(o, ch).wait_send()
    for o in range(1, dp):
        cot_copy(o).wait_send()
        n_copy(o).wait_send()
        for ch in range(chunks):
            w_copy(o, ch).wait_send()
            for g in range(groups):
                forward_copy(o, ch, g).wait_send()
    for o in range(dp):
        c = d_at(o)
        for j in range(per_dp):
            if o:
                g_copy(c, j).wait_send()
            else:
                @pl.when(d * per_dp + j != z)
                def _():
                    g_copy(c, j).wait_send()


def on_device(
    layer_inputs, ln_gain, ln_bias, qkv_weight, out_weight, dec_embed, decoder_grad, previous, visible
):
    dp = lax.axis_size("dp")
    segs = lax.axis_size("segment")
    groups = lax.axis_size("seq")
    tokens = layer_inputs[0, 0]
    tok, width = tokens.shape
    head_size = width // HEADS
    head_count = HEADS // groups
    pair = 2 if head_count % 2 == 0 else 1
    chunks = head_count // pair
    cw = pair * head_size
    depth = width // dp
    per_dp = groups // dp
    patches, dec = decoder_grad.shape[1:]
    sliced = cw % 128 == 0
    weight = qkv_weight[0]
    if not sliced:
        weight = weight.reshape(depth, 3, groups, chunks, cw).transpose(2, 3, 0, 1, 4)
        weight = weight.reshape(groups, chunks, depth, 3 * cw)
    dims = (dp, segs, groups, tok, width, chunks, pair, head_size, sliced)
    vmem = pl.BlockSpec(memory_space=pltpu.VMEM)
    anywhere = pl.BlockSpec(memory_space=pl.ANY)
    dma = pltpu.SemaphoreType.DMA
    result = pl.pallas_call(
        functools.partial(kernel, dims),
        out_shape=jax.ShapeDtypeStruct((tok, width), BF16),
        in_specs=[vmem] * 5 + [anywhere] * 4,
        out_specs=vmem,
        scratch_shapes=[
            pltpu.VMEM((groups, chunks, depth, 3 * cw), BF16),
            pltpu.VMEM((dp, chunks, depth, 3 * cw), BF16),
            pltpu.VMEM((depth, width), BF16),
            pltpu.VMEM((width, dec), BF16),
            pltpu.VMEM((patches, dec), BF16),
            pltpu.VMEM((groups, tok, width), BF16),
            pltpu.VMEM((tok, width), F32),
            pltpu.VMEM((tok, 128), F32),
            pltpu.VMEM((dp, tok, width), BF16),
            pltpu.VMEM((dp, per_dp, chunks, tok, cw), BF16),
            pltpu.VMEM((groups, chunks, tok, cw), BF16),
            pltpu.VMEM((groups, tok, dec), BF16),
            pltpu.VMEM((groups, tok, dec), BF16),
            pltpu.VMEM((groups * tok, 3 * cw), BF16),
            pltpu.VMEM((chunks, groups, tok, 3 * cw), BF16),
            pltpu.VMEM((chunks, dp, groups, tok, 3 * cw), BF16),
            pltpu.VMEM((dp, tok, depth), F32),
            pltpu.VMEM((dp, tok, depth), F32),
            dma((groups, chunks, 3)),
            dma((3,)),
            dma((1,)),
            dma((1,)),
            dma((dp, chunks)),
            dma((dp, chunks)),
            dma((groups,)),
            dma((groups,)),
            dma((groups,)),
            dma((groups,)),
            dma((dp,)),
            dma((dp,)),
            dma((dp, per_dp)),
            dma((groups,)),
            dma((chunks, groups)),
            dma((chunks, groups)),
            dma((chunks, dp, groups)),
            dma((chunks, dp, groups)),
            dma((dp,)),
            dma((dp,)),
        ],
        compiler_params=pltpu.CompilerParams(
            collective_id=0, has_side_effects=True, vmem_limit_bytes=56 * 1024 * 1024
        ),
    )(
        tokens,
        ln_gain,
        ln_bias,
        previous[0, 0],
        visible[0].reshape(groups, 1, tok),
        weight,
        out_weight[0],
        dec_embed,
        decoder_grad[0],
    )
    return result[None, None]


def solution(mesh):
    placed = (
        P("segment", "dp", "seq", None),
        P("segment", None),
        P("segment", None),
        P("segment", "dp", None),
        P("segment", "dp", None),
        P(),
        P("dp", "seq", None),
        P("segment", "dp", "seq", None),
        P("dp", None),
    )
    return jax.shard_map(
        on_device,
        mesh=mesh,
        in_specs=placed,
        out_specs=P("segment", "dp", "seq", None),
        check_vma=False,
    )
```

time: 322 us -> 86.5 us (0.27)
  the two profiles are of different devices: /device:TPU:0 before, /device:TPU:13 now
where the time goes in v1:
time: 86.5 us; the launch traced here: 86.3 us
  Pallas kernels  84.6 us (98%)
  local copies, waits for them, and re-layouts  1.67 us (2%)
    pallas_call x1, Pallas kernels, on_device(): pl.pallas_call(functools.partial(kernel, dims), out_shape=jax.ShapeDtypeS...  84.6 us

profile of v1, /device:TPU:13, one launch (start us, length us, event | category | flops | bytes accessed | tf_op | source)
XLA Modules:
  0.0 86.3 jit_solution(6961776239583558037)
XLA Ops:
  0.0 84.6 %shard_map.91 = bf16[128,1024]{1,0:T(8,128)(2,1)} custom-call(bf16[128,1024]{1,0:T(8,128)(2,1)} %bitcast.11, f32[1,1024]{1,0:T(1,128)} %gain_ref.1, f32[1,1024]{1,0:T(1,128)} %bias_ref.1, bf16[128,1024]{1,0:T(8,128)(2,1)} %bitcast.12, s32[4,1,128]{2,1,0:T(1,128)} %bitcast.13, bf16[512,3072]{1,0:T(8,128)(2,1)} %bitcast.7, bf16[512,1024]{1,0:T(8,128)(2,1)} %bitcast.9, ...), custom_call_target="tpu_custom_call" | custom-call | tf_op jit(solution)/shard_map/pallas_call | solution.py:389
  84.6 1.7 %copy.11 = bf16[1,1,128,1024]{3,2,1,0:T(8,128)(2,1)} copy(bf16[1,1,128,1024]{3,2,1,0:T(8,128)(2,1)} %bitcast.8) | data formatting | bytes 524288

commit v2 on v1

--- a/solution.py
+++ b/solution.py
@@ -57,10 +57,10 @@
     dims,
     x_ref, gain_ref, bias_ref, prev_ref, ids_ref, w_ref, ow_ref, de_ref, dg_ref,
     out_ref,
-    wg, wc, ow, de, dg, low, normed_ref, spread_ref, cot, go, ga, pk, pr,
-    pj, gp, rb, gns, gnr,
-    lw_sem, lo_sem, prev_s, prev_r, w_s, w_r, pk_s, pk_r, l_s, l_r, ct_s, ct_r,
-    g_s, g_r, b_s, b_r, f_s, f_r, n_s, n_r,
+    wc, ow, de, dg, low, normed_ref, spread_ref, cot, go, ga, pk, pr, px,
+    pj, gp, ps, pn,
+    lw_sem, lo_sem, prev_s, prev_r, w_s, w_r, pk_s, pk_r, px_s, px_r, l_s, l_r,
+    g_s, g_r, b_s, b_r,
 ):
     dp, segs, groups, tok, width, chunks, pair, head_size, sliced = dims
     cw = pair * head_size
@@ -85,28 +85,24 @@
             device_id=(dd, ss, zz), device_id_type=MESH,
         )
 
-    def w_copies(o):
-        g = z_at(o)
-        if not sliced:
-            return [pltpu.make_async_copy(w_ref.at[g], wg.at[g], lw_sem.at[o, 0, 0])]
-        found = []
+    local_w = []
+    if sliced:
         for ch in range(chunks):
             for part in range(3):
-                at = pl.multiple_of(part * width + g * hw + ch * cw, 128)
-                found.append(
+                at = pl.multiple_of(part * width + z * hw + ch * cw, 128)
+                local_w.append(
                     pltpu.make_async_copy(
                         w_ref.at[:, pl.ds(at, cw)],
-                        wg.at[g, ch, :, pl.ds(part * cw, cw)],
-                        lw_sem.at[o, ch, part],
+                        wc.at[d, ch, :, pl.ds(part * cw, cw)],
+                        lw_sem.at[ch, part],
                     )
                 )
-        return found
-
-    local_w = [w_copies(o) for o in range(groups)]
+    else:
+        local_w.append(pltpu.make_async_copy(w_ref.at[z], wc.at[d], lw_sem.at[0, 0]))
     ow_copy = pltpu.make_async_copy(ow_ref, ow, lo_sem.at[0])
     de_copy = pltpu.make_async_copy(de_ref, de, lo_sem.at[1])
     dg_copy = pltpu.make_async_copy(dg_ref, dg, lo_sem.at[2])
-    for copy in local_w[0]:
+    for copy in local_w:
         copy.start()
 
     @pl.when(last)
@@ -115,9 +111,6 @@
         de_copy.start()
 
     ow_copy.start()
-    for o in range(1, groups):
-        for copy in local_w[o]:
-            copy.start()
 
     barrier = pltpu.get_barrier_semaphore()
     for od in range(dp):
@@ -127,17 +120,22 @@
                     barrier, inc=1, device_id=(d_at(od), s, z_at(oz)), device_id_type=MESH
                 )
 
-    pl.semaphore_signal(
-        barrier, inc=1, device_id=(d, lax.rem(s + 1, segs), z), device_id_type=MESH
-    )
-    pl.semaphore_wait(barrier, dp * groups)
+    for od in range(dp):
+        pl.semaphore_signal(
+            barrier, inc=1, device_id=(d_at(od), lax.rem(s + 1, segs), z), device_id_type=MESH
+        )
+    pl.semaphore_wait(barrier, dp * groups - 1 + dp)
 
     down = jnp.maximum(s - 1, 0)
-    prev_copy = remote(prev_ref, cot.at[d], prev_s.at[0], prev_r.at[0], d, down, z)
+
+    def prev_copy(o):
+        c = d_at(o)
+        return remote(prev_ref, cot.at[d], prev_s.at[c], prev_r.at[d], c, down, z)
 
     @pl.when(s > 0)
     def _():
-        prev_copy.start()
+        for o in range(dp):
+            prev_copy(o).start()
 
     def pick_copy(o):
         g = z_at(o)
@@ -177,17 +175,16 @@
 
     def w_copy(o, ch):
         dd = d_at(o)
-        return remote(wg.at[z, ch], wc.at[d, ch], w_s.at[dd, ch], w_r.at[d, ch], dd, s, z)
-
-    for copy in local_w[0]:
+        return remote(wc.at[d, ch], wc.at[d, ch], w_s.at[dd, ch], w_r.at[d, ch], dd, s, z)
+
+    for copy in local_w:
         copy.wait()
     for ch in range(chunks):
         for o in range(1, dp):
             w_copy(o, ch).start()
 
-    @pl.when(s < segs - 1)
-    def _():
-        prev_copy.wait_recv()
+    def px_copy(o):
+        return remote(px.at[d], px.at[d], px_s.at[d_at(o)], px_r.at[d], d_at(o), s, z)
 
     @pl.when(last)
     def _():
@@ -196,14 +193,10 @@
         picked = pr[0].astype(F32)
         for g in range(1, groups):
             picked = picked + pr[g].astype(F32)
+        px[d] = picked.astype(BF16)
+        for o in range(1, dp):
+            px_copy(o).start()
         de_copy.wait()
-        cot[d] = contract_last(picked.astype(BF16), de[...]).astype(BF16)
-
-    def cot_copy(o):
-        return remote(cot.at[d], cot.at[d], ct_s.at[d_at(o)], ct_r.at[d], d_at(o), s, z)
-
-    for o in range(1, dp):
-        cot_copy(o).start()
 
     def g_copy(c, j):
         g = d * per_dp + j
@@ -212,8 +205,19 @@
     ow_copy.wait()
     for o in range(dp):
         c = d_at(o)
-        if o:
-            arrive(cot.at[c], ct_r.at[c], c, z)
+
+        @pl.when(s < segs - 1)
+        def _():
+            remote(
+                prev_ref, cot.at[c], prev_s.at[c], prev_r.at[c], c, lax.rem(s + 1, segs), z
+            ).wait_recv()
+
+        @pl.when(last)
+        def _():
+            if o:
+                arrive(px.at[c], px_r.at[c], c, z)
+            cot[c] = contract_last(px[c], de[...]).astype(BF16)
+
         grads = contract_last(cot[c], ow[...]).astype(BF16)
         for j in range(per_dp):
             for ch in range(chunks):
@@ -232,22 +236,9 @@
                 def _():
                     ga[z] = go[c, j]
 
-    def back_copy(o, ch):
+    def back_copy(o):
         g = z_at(o)
-        return remote(gp.at[ch, g], rb.at[ch, d, z], b_s.at[ch, g], b_r.at[ch, z], d, s, g)
-
-    def forward_copy(o, ch, g):
-        dd = d_at(o)
-        return remote(
-            rb.at[ch, d, g], rb.at[ch, d, g], f_s.at[ch, dd, g], f_r.at[ch, d, g], dd, s, z
-        )
-
-    def forward(ch):
-        for o in range(1, groups):
-            g = z_at(o)
-            arrive(rb.at[ch, d, g], b_r.at[ch, g], d, g)
-            for od in range(1, dp):
-                forward_copy(od, ch, g).start()
+        return remote(ps.at[g], pn.at[z], b_s.at[g], b_r.at[z], d, s, g)
 
     scaling = head_size ** (-0.5)
     for ch in range(chunks):
@@ -259,7 +250,7 @@
             dd = d_at(o)
             if o:
                 arrive(wc.at[dd, ch], w_r.at[dd, ch], dd, z)
-            weights = wc[dd, ch] if o else wg[z, ch]
+            weights = wc[dd, ch]
             columns = low[:, :, pl.ds(pl.multiple_of(dd * depth, depth), depth)]
             term = jnp.dot(
                 columns.reshape(groups * tok, depth), weights, preferred_element_type=F32
@@ -286,41 +277,24 @@
         for part in range(3):
             whole = found[part][0] if pair == 1 else jnp.concatenate(found[part], axis=1)
             gp[ch, :, :, part * cw : (part + 1) * cw] = whole.reshape(groups, tok, cw)
-        for o in range(1, groups):
-            back_copy(o, ch).start()
-        rb[ch, d, z] = gp[ch, z]
-        for od in range(1, dp):
-            forward_copy(od, ch, z).start()
-        if ch:
-            forward(ch - 1)
-    forward(chunks - 1)
+
+    def term(g, c):
+        total = None
+        for ch in range(chunks):
+            part = contract_last(gp[ch, g], wc[c, ch])
+            total = part if total is None else total + part
+        return total
+
     for o in range(1, groups):
-        for copy in local_w[o]:
-            copy.wait()
-
-    def half(c):
-        def step(g, total):
-            for ch in range(chunks):
-                total = total + contract_last(rb[ch, c, g], wg[g, ch])
-            return total
-
-        return lax.fori_loop(0, groups, step, jnp.zeros((tok, depth), F32))
-
-    def n_copy(o):
-        c = d_at(o)
-        return remote(gns.at[c], gnr.at[d], n_s.at[c], n_r.at[d], c, s, z)
-
-    gnr[d] = half(d)
-    for o in range(1, dp):
-        c = d_at(o)
-        for ch in range(chunks):
-            for g in range(groups):
-                arrive(rb.at[ch, c, g], f_r.at[ch, c, g], c, z)
-        gns[c] = half(c)
-        n_copy(o).start()
-    for o in range(1, dp):
-        arrive(gnr.at[d_at(o)], n_r.at[d_at(o)], d_at(o), z)
-    grad_norm = jnp.concatenate([gnr[c] for c in range(dp)], axis=1)
+        g = z_at(o)
+        for c in range(dp):
+            ps[g, :, c * depth : (c + 1) * depth] = term(g, c).astype(BF16)
+        back_copy(o).start()
+    grad_norm = jnp.concatenate([term(z, c) for c in range(dp)], axis=1)
+    for o in range(1, groups):
+        g = z_at(o)
+        arrive(pn.at[g], b_r.at[g], d, g)
+        grad_norm = grad_norm + pn[g].astype(F32)
     scaled = grad_norm * gain_ref[...]
     normed = normed_ref[...]
     grad_in = (
@@ -332,24 +306,22 @@
 
     @pl.when(s > 0)
     def _():
-        prev_copy.wait_send()
+        for o in range(dp):
+            prev_copy(o).wait_send()
 
     @pl.when(last)
     def _():
         for o in range(1, groups):
             pick_copy(o).wait_send()
+        for o in range(1, dp):
+            px_copy(o).wait_send()
 
     for o in range(1, groups):
         low_copy(o).wait_send()
-        for ch in range(chunks):
-            back_copy(o, ch).wait_send()
+        back_copy(o).wait_send()
     for o in range(1, dp):
-        cot_copy(o).wait_send()
-        n_copy(o).wait_send()
         for ch in range(chunks):
             w_copy(o, ch).wait_send()
-            for g in range(groups):
-                forward_copy(o, ch, g).wait_send()
     for o in range(dp):
         c = d_at(o)
         for j in range(per_dp):
@@ -392,7 +364,6 @@
         in_specs=[vmem] * 5 + [anywhere] * 4,
         out_specs=vmem,
         scratch_shapes=[
-            pltpu.VMEM((groups, chunks, depth, 3 * cw), BF16),
             pltpu.VMEM((dp, chunks, depth, 3 * cw), BF16),
             pltpu.VMEM((depth, width), BF16),
             pltpu.VMEM((width, dec), BF16),
@@ -405,31 +376,27 @@
             pltpu.VMEM((groups, chunks, tok, cw), BF16),
             pltpu.VMEM((groups, tok, dec), BF16),
             pltpu.VMEM((groups, tok, dec), BF16),
+            pltpu.VMEM((dp, tok, dec), BF16),
             pltpu.VMEM((groups * tok, 3 * cw), BF16),
             pltpu.VMEM((chunks, groups, tok, 3 * cw), BF16),
-            pltpu.VMEM((chunks, dp, groups, tok, 3 * cw), BF16),
-            pltpu.VMEM((dp, tok, depth), F32),
-            pltpu.VMEM((dp, tok, depth), F32),
-            dma((groups, chunks, 3)),
+            pltpu.VMEM((groups, tok, width), BF16),
+            pltpu.VMEM((groups, tok, width), BF16),
+            dma((chunks, 3)),
             dma((3,)),
-            dma((1,)),
-            dma((1,)),
+            dma((dp,)),
+            dma((dp,)),
             dma((dp, chunks)),
             dma((dp, chunks)),
             dma((groups,)),
             dma((groups,)),
-            dma((groups,)),
-            dma((groups,)),
             dma((dp,)),
             dma((dp,)),
+            dma((groups,)),
+            dma((groups,)),
             dma((dp, per_dp)),
             dma((groups,)),
-            dma((chunks, groups)),
-            dma((chunks, groups)),
-            dma((chunks, dp, groups)),
-            dma((chunks, dp, groups)),
-            dma((dp,)),
-            dma((dp,)),
+            dma((groups,)),
+            dma((groups,)),
         ],
         compiler_params=pltpu.CompilerParams(
             collective_id=0, has_side_effects=True, vmem_limit_bytes=56 * 1024 * 1024

time: 86.5 us -> 79.8 us (0.923)
  Pallas kernels: 84.6 us -> 78 us
    pallas_call x1, Pallas kernels: 84.6 us -> 78 us  [on_device(): pl.pallas_call(functools.partial(kernel, dims), out_shape=jax.ShapeDtypeS...]
where the time goes in v2:
time: 79.8 us; the launch traced here: 79.7 us
  Pallas kernels  78 us (98%)
  local copies, waits for them, and re-layouts  1.67 us (2%)
    pallas_call x1, Pallas kernels, on_device(): pl.pallas_call(functools.partial(kernel, dims), out_shape=jax.ShapeDtypeS...  78 us
    unnamed x1, local copies, waits for them, and re-layouts  1.67 us

profile of v2, /device:TPU:13, one launch (start us, length us, event | category | flops | bytes accessed | tf_op | source)
XLA Modules:
  0.0 79.7 jit_solution(3803093804778151511)
XLA Ops:
  0.0 78.0 %shard_map.91 = bf16[128,1024]{1,0:T(8,128)(2,1)} custom-call(bf16[128,1024]{1,0:T(8,128)(2,1)} %bitcast.11, f32[1,1024]{1,0:T(1,128)} %gain_ref.1, f32[1,1024]{1,0:T(1,128)} %bias_ref.1, bf16[128,1024]{1,0:T(8,128)(2,1)} %bitcast.12, s32[4,1,128]{2,1,0:T(1,128)} %bitcast.13, bf16[512,3072]{1,0:T(8,128)(2,1)} %bitcast.7, bf16[512,1024]{1,0:T(8,128)(2,1)} %bitcast.9, ...), custom_call_target="tpu_custom_call" | custom-call | tf_op jit(solution)/shard_map/pallas_call | solution.py:361
  78.0 1.7 %copy.11 = bf16[1,1,128,1024]{3,2,1,0:T(8,128)(2,1)} copy(bf16[1,1,128,1024]{3,2,1,0:T(8,128)(2,1)} %bitcast.8) | data formatting | bytes 524288

commit v3 on v2

--- a/solution.py
+++ b/solution.py
@@ -58,7 +58,7 @@
     x_ref, gain_ref, bias_ref, prev_ref, ids_ref, w_ref, ow_ref, de_ref, dg_ref,
     out_ref,
     wc, ow, de, dg, low, normed_ref, spread_ref, cot, go, ga, pk, pr, px,
-    pj, gp, ps, pn,
+    pa, pj, gp, ps, pn,
     lw_sem, lo_sem, prev_s, prev_r, w_s, w_r, pk_s, pk_r, px_s, px_r, l_s, l_r,
     g_s, g_r, b_s, b_r,
 ):
@@ -165,13 +165,23 @@
     normed = center / spread
     normed_ref[...] = normed
     spread_ref[...] = jnp.broadcast_to(spread, spread_ref.shape)
-    low[z] = (normed * gain_ref[...] + bias_ref[...]).astype(BF16)
-
-    def low_copy(o):
-        return remote(low.at[z], low.at[z], l_s.at[z_at(o)], l_r.at[z], d, s, z_at(o))
+    lowered = (normed * gain_ref[...] + bias_ref[...]).astype(BF16)
+    for c in range(dp):
+        low[z, c] = lowered[:, c * depth : (c + 1) * depth]
+
+    def low_copy(o, p):
+        c = d_at(p)
+        return remote(
+            low.at[z, c], low.at[z, c], l_s.at[z_at(o), c], l_r.at[z, c], d, s, z_at(o)
+        )
+
+    def low_arrive(p):
+        c = d_at(p)
+        for o in range(1, groups):
+            arrive(low.at[z_at(o), c], l_r.at[z_at(o), c], d, z_at(o))
 
     for o in range(1, groups):
-        low_copy(o).start()
+        low_copy(o, 0).start()
 
     def w_copy(o, ch):
         dd = d_at(o)
@@ -179,9 +189,11 @@
 
     for copy in local_w:
         copy.wait()
-    for ch in range(chunks):
-        for o in range(1, dp):
-            w_copy(o, ch).start()
+
+    @pl.when(s < segs - 1)
+    def _():
+        for o in range(1, dp):
+            w_copy(o, 0).start()
 
     def px_copy(o):
         return remote(px.at[d], px.at[d], px_s.at[d_at(o)], px_r.at[d], d_at(o), s, z)
@@ -196,6 +208,8 @@
         px[d] = picked.astype(BF16)
         for o in range(1, dp):
             px_copy(o).start()
+        for o in range(1, dp):
+            w_copy(o, 0).start()
         de_copy.wait()
 
     def g_copy(c, j):
@@ -236,26 +250,33 @@
                 def _():
                     ga[z] = go[c, j]
 
+    for p in range(1, dp):
+        for o in range(1, groups):
+            low_copy(o, p).start()
+    for ch in range(1, chunks):
+        for o in range(1, dp):
+            w_copy(o, ch).start()
+    low_arrive(0)
+    for ch in range(chunks):
+        pa[ch] = jnp.dot(
+            low[:, d].reshape(groups * tok, depth), wc[d, ch], preferred_element_type=F32
+        )
+
     def back_copy(o):
         g = z_at(o)
         return remote(ps.at[g], pn.at[z], b_s.at[g], b_r.at[z], d, s, g)
 
     scaling = head_size ** (-0.5)
     for ch in range(chunks):
-        if ch == 0:
-            for o in range(1, groups):
-                arrive(low.at[z_at(o)], l_r.at[z_at(o)], d, z_at(o))
-        total = None
-        for o in range(dp):
+        total = pa[ch]
+        for o in range(1, dp):
             dd = d_at(o)
-            if o:
-                arrive(wc.at[dd, ch], w_r.at[dd, ch], dd, z)
-            weights = wc[dd, ch]
-            columns = low[:, :, pl.ds(pl.multiple_of(dd * depth, depth), depth)]
-            term = jnp.dot(
-                columns.reshape(groups * tok, depth), weights, preferred_element_type=F32
+            if ch == 0:
+                low_arrive(o)
+            arrive(wc.at[dd, ch], w_r.at[dd, ch], dd, z)
+            total = total + jnp.dot(
+                low[:, dd].reshape(groups * tok, depth), wc[dd, ch], preferred_element_type=F32
             )
-            total = term if total is None else total + term
         pj[...] = total.astype(BF16)
         if ch == 0:
             for src in range(groups):
@@ -317,7 +338,8 @@
             px_copy(o).wait_send()
 
     for o in range(1, groups):
-        low_copy(o).wait_send()
+        for p in range(dp):
+            low_copy(o, p).wait_send()
         back_copy(o).wait_send()
     for o in range(1, dp):
         for ch in range(chunks):
@@ -368,7 +390,7 @@
             pltpu.VMEM((depth, width), BF16),
             pltpu.VMEM((width, dec), BF16),
             pltpu.VMEM((patches, dec), BF16),
-            pltpu.VMEM((groups, tok, width), BF16),
+            pltpu.VMEM((groups, dp, tok, depth), BF16),
             pltpu.VMEM((tok, width), F32),
             pltpu.VMEM((tok, 128), F32),
             pltpu.VMEM((dp, tok, width), BF16),
@@ -377,6 +399,7 @@
             pltpu.VMEM((groups, tok, dec), BF16),
             pltpu.VMEM((groups, tok, dec), BF16),
             pltpu.VMEM((dp, tok, dec), BF16),
+            pltpu.VMEM((chunks, groups * tok, 3 * cw), F32),
             pltpu.VMEM((groups * tok, 3 * cw), BF16),
             pltpu.VMEM((chunks, groups, tok, 3 * cw), BF16),
             pltpu.VMEM((groups, tok, width), BF16),
@@ -391,8 +414,8 @@
             dma((groups,)),
             dma((dp,)),
             dma((dp,)),
-            dma((groups,)),
-            dma((groups,)),
+            dma((groups, dp)),
+            dma((groups, dp)),
             dma((dp, per_dp)),
             dma((groups,)),
             dma((groups,)),

time: 79.8 us -> 79.2 us (level); the launches traced: 79.7 us -> 78.1 us
  Pallas kernels: 78 us -> 76.4 us
    pallas_call x1, Pallas kernels: 78 us -> 76.4 us  [on_device(): pl.pallas_call(functools.partial(kernel, dims), out_shape=jax.ShapeDtypeS...]
where the time goes in v3:
time: 79.2 us; the launch traced here: 78.1 us
  Pallas kernels  76.4 us (96%)
  local copies, waits for them, and re-layouts  1.67 us (2%)
    pallas_call x1, Pallas kernels, on_device(): pl.pallas_call(functools.partial(kernel, dims), out_shape=jax.ShapeDtypeS...  76.4 us
    unnamed x1, local copies, waits for them, and re-layouts  1.67 us

profile of v3, /device:TPU:13, one launch (start us, length us, event | category | flops | bytes accessed | tf_op | source)
XLA Modules:
  0.0 78.1 jit_solution(17100582426189440750)
XLA Ops:
  0.0 76.4 %shard_map.91 = bf16[128,1024]{1,0:T(8,128)(2,1)} custom-call(bf16[128,1024]{1,0:T(8,128)(2,1)} %bitcast.11, f32[1,1024]{1,0:T(1,128)} %gain_ref.1, f32[1,1024]{1,0:T(1,128)} %bias_ref.1, bf16[128,1024]{1,0:T(8,128)(2,1)} %bitcast.12, s32[4,1,128]{2,1,0:T(1,128)} %bitcast.13, bf16[512,3072]{1,0:T(8,128)(2,1)} %bitcast.7, bf16[512,1024]{1,0:T(8,128)(2,1)} %bitcast.9, ...), custom_call_target="tpu_custom_call" | custom-call | tf_op jit(solution)/shard_map/pallas_call | solution.py:383
  76.5 1.7 %copy.11 = bf16[1,1,128,1024]{3,2,1,0:T(8,128)(2,1)} copy(bf16[1,1,128,1024]{3,2,1,0:T(8,128)(2,1)} %bitcast.8) | data formatting | bytes 524288

commit v4 on v3

--- a/solution.py
+++ b/solution.py
@@ -124,6 +124,16 @@
         pl.semaphore_signal(
             barrier, inc=1, device_id=(d_at(od), lax.rem(s + 1, segs), z), device_id_type=MESH
         )
+    values = x_ref[...].astype(F32)
+    center = values - jnp.mean(values, axis=1, keepdims=True)
+    spread = jnp.sqrt(jnp.mean(center * center, axis=1, keepdims=True) + EPS)
+    normed = center / spread
+    normed_ref[...] = normed
+    spread_ref[...] = jnp.broadcast_to(spread, spread_ref.shape)
+    lowered = (normed * gain_ref[...] + bias_ref[...]).astype(BF16)
+    for c in range(dp):
+        low[z, c] = lowered[:, c * depth : (c + 1) * depth]
+
     pl.semaphore_wait(barrier, dp * groups - 1 + dp)
 
     down = jnp.maximum(s - 1, 0)
@@ -159,29 +169,35 @@
             else:
                 pr[z] = rows
 
-    values = x_ref[...].astype(F32)
-    center = values - jnp.mean(values, axis=1, keepdims=True)
-    spread = jnp.sqrt(jnp.mean(center * center, axis=1, keepdims=True) + EPS)
-    normed = center / spread
-    normed_ref[...] = normed
-    spread_ref[...] = jnp.broadcast_to(spread, spread_ref.shape)
-    lowered = (normed * gain_ref[...] + bias_ref[...]).astype(BF16)
-    for c in range(dp):
-        low[z, c] = lowered[:, c * depth : (c + 1) * depth]
-
-    def low_copy(o, p):
+    def low_copy(src, p, way):
         c = d_at(p)
         return remote(
-            low.at[z, c], low.at[z, c], l_s.at[z_at(o), c], l_r.at[z, c], d, s, z_at(o)
+            low.at[src, c], low.at[src, c], l_s.at[way, src, c], l_r.at[src, c],
+            d, s, z + 1 - 2 * way,
         )
 
-    def low_arrive(p):
-        c = d_at(p)
-        for o in range(1, groups):
-            arrive(low.at[z_at(o), c], l_r.at[z_at(o), c], d, z_at(o))
-
-    for o in range(1, groups):
-        low_copy(o, 0).start()
+    def low_step(p, way, k, act):
+        src = z - k if way == 0 else z + k
+        here = src >= 0 if way == 0 else src < groups
+        onward = z < groups - 1 if way == 0 else z > 0
+        if k and act == "start":
+            @pl.when(here)
+            def _():
+                arrive(low.at[src, d_at(p)], l_r.at[src, d_at(p)], d, src)
+
+        @pl.when(jnp.logical_and(here, onward))
+        def _():
+            if act == "start":
+                low_copy(src, p, way).start()
+            else:
+                low_copy(src, p, way).wait_send()
+
+    def low_relay(k, act="start"):
+        for p in range(dp):
+            for way in range(2):
+                low_step(p, way, k, act)
+
+    low_relay(0)
 
     def w_copy(o, ch):
         dd = d_at(o)
@@ -211,6 +227,8 @@
         for o in range(1, dp):
             w_copy(o, 0).start()
         de_copy.wait()
+
+    low_relay(1)
 
     def g_copy(c, j):
         g = d * per_dp + j
@@ -250,13 +268,11 @@
                 def _():
                     ga[z] = go[c, j]
 
-    for p in range(1, dp):
-        for o in range(1, groups):
-            low_copy(o, p).start()
     for ch in range(1, chunks):
         for o in range(1, dp):
             w_copy(o, ch).start()
-    low_arrive(0)
+    for k in range(2, groups):
+        low_relay(k)
     for ch in range(chunks):
         pa[ch] = jnp.dot(
             low[:, d].reshape(groups * tok, depth), wc[d, ch], preferred_element_type=F32
@@ -271,8 +287,6 @@
         total = pa[ch]
         for o in range(1, dp):
             dd = d_at(o)
-            if ch == 0:
-                low_arrive(o)
             arrive(wc.at[dd, ch], w_r.at[dd, ch], dd, z)
             total = total + jnp.dot(
                 low[:, dd].reshape(groups * tok, depth), wc[dd, ch], preferred_element_type=F32
@@ -338,9 +352,9 @@
             px_copy(o).wait_send()
 
     for o in range(1, groups):
-        for p in range(dp):
-            low_copy(o, p).wait_send()
         back_copy(o).wait_send()
+    for k in range(groups - 1):
+        low_relay(k, 'wait')
     for o in range(1, dp):
         for ch in range(chunks):
             w_copy(o, ch).wait_send()
@@ -383,7 +397,7 @@
     result = pl.pallas_call(
         functools.partial(kernel, dims),
         out_shape=jax.ShapeDtypeStruct((tok, width), BF16),
-        in_specs=[vmem] * 5 + [anywhere] * 4,
+        in_specs=[vmem] * 3 + [anywhere, vmem] + [anywhere] * 4,
         out_specs=vmem,
         scratch_shapes=[
             pltpu.VMEM((dp, chunks, depth, 3 * cw), BF16),
@@ -414,7 +428,7 @@
             dma((groups,)),
             dma((dp,)),
             dma((dp,)),
-            dma((groups, dp)),
+            dma((2, groups, dp)),
             dma((groups, dp)),
             dma((dp, per_dp)),
             dma((groups,)),

time: 79.2 us -> 68 us (0.86); the launches traced: 78.1 us -> 67.8 us
  Pallas kernels: 76.4 us -> 66.2 us
    pallas_call x1, Pallas kernels: 76.4 us -> 66.2 us  [on_device(): pl.pallas_call(functools.partial(kernel, dims), out_shape=jax.ShapeDtypeS...]
where the time goes in v4:
time: 68 us; the launch traced here: 67.8 us
  Pallas kernels  66.2 us (97%)
  local copies, waits for them, and re-layouts  1.67 us (2%)
    pallas_call x1, Pallas kernels, on_device(): pl.pallas_call(functools.partial(kernel, dims), out_shape=jax.ShapeDtypeS...  66.2 us
    unnamed x1, local copies, waits for them, and re-layouts  1.67 us

profile of v4, /device:TPU:13, one launch (start us, length us, event | category | flops | bytes accessed | tf_op | source)
XLA Modules:
  0.0 67.8 jit_solution(7143304604993526192)
XLA Ops:
  0.0 66.2 %shard_map.91 = bf16[128,1024]{1,0:T(8,128)(2,1)} custom-call(bf16[128,1024]{1,0:T(8,128)(2,1)} %bitcast.11, f32[1,1024]{1,0:T(1,128)} %gain_ref.1, f32[1,1024]{1,0:T(1,128)} %bias_ref.1, bf16[128,1024]{1,0:T(8,128)(2,1)} %bitcast.12, s32[4,1,128]{2,1,0:T(1,128)} %bitcast.13, bf16[512,3072]{1,0:T(8,128)(2,1)} %bitcast.7, bf16[512,1024]{1,0:T(8,128)(2,1)} %bitcast.9, ...), custom_call_target="tpu_custom_call" | custom-call | tf_op jit(solution)/shard_map/pallas_call | solution.py:397
  66.2 1.7 %copy.11 = bf16[1,1,128,1024]{3,2,1,0:T(8,128)(2,1)} copy(bf16[1,1,128,1024]{3,2,1,0:T(8,128)(2,1)} %bitcast.8) | data formatting | bytes 524288

commit v5 on v4

--- a/solution.py
+++ b/solution.py
@@ -124,6 +124,29 @@
         pl.semaphore_signal(
             barrier, inc=1, device_id=(d_at(od), lax.rem(s + 1, segs), z), device_id_type=MESH
         )
+    def meets(block, g):
+        few, most, rows = tok // 8, 15 * tok // 8, groups * tok
+        first = jnp.maximum(block * few, rows - (groups - block) * most)
+        end = jnp.minimum((block + 1) * most, rows - (groups - 1 - block) * few)
+        return jnp.logical_and(first < (g + 1) * tok, end > g * tok)
+
+    @pl.when(last)
+    def _():
+        dg_copy.wait()
+        patches = dg.shape[0]
+        patch_ids = lax.broadcasted_iota(jnp.int32, (patches, tok), 0) + z * patches
+        for o in list(range(1, groups)) + [0]:
+            g = z_at(o)
+
+            @pl.when(meets(z, g))
+            def _():
+                hit = jnp.where(patch_ids == ids_ref[g], 1.0, 0.0).astype(BF16)
+                rows = contract_first(hit, dg[...]).astype(BF16)
+                if o:
+                    pk[g] = rows
+                else:
+                    pr[z] = rows
+
     values = x_ref[...].astype(F32)
     center = values - jnp.mean(values, axis=1, keepdims=True)
     spread = jnp.sqrt(jnp.mean(center * center, axis=1, keepdims=True) + EPS)
@@ -156,18 +179,10 @@
 
     @pl.when(last)
     def _():
-        dg_copy.wait()
-        patches = dg.shape[0]
-        patch_ids = lax.broadcasted_iota(jnp.int32, (patches, tok), 0) + z * patches
-        for o in list(range(1, groups)) + [0]:
-            g = z_at(o)
-            hit = jnp.where(patch_ids == ids_ref[g], 1.0, 0.0).astype(BF16)
-            rows = contract_first(hit, dg[...]).astype(BF16)
-            if o:
-                pk[g] = rows
+        for o in range(1, groups):
+            @pl.when(meets(z, z_at(o)))
+            def _():
                 pick_copy(o).start()
-            else:
-                pr[z] = rows
 
     def low_copy(src, p, way):
         c = d_at(p)
@@ -217,7 +232,16 @@
     @pl.when(last)
     def _():
         for o in range(1, groups):
-            arrive(pr.at[z_at(o)], pk_r.at[z_at(o)], d, z_at(o))
+            g = z_at(o)
+
+            @pl.when(meets(g, z))
+            def _():
+                arrive(pr.at[g], pk_r.at[g], d, g)
+
+            @pl.when(jnp.logical_not(meets(g, z)))
+            def _():
+                pr[g] = jnp.zeros(pr.shape[1:], BF16)
+
         picked = pr[0].astype(F32)
         for g in range(1, groups):
             picked = picked + pr[g].astype(F32)
@@ -347,7 +371,10 @@
     @pl.when(last)
     def _():
         for o in range(1, groups):
-            pick_copy(o).wait_send()
+            @pl.when(meets(z, z_at(o)))
+            def _():
+                pick_copy(o).wait_send()
+
         for o in range(1, dp):
             px_copy(o).wait_send()
 

time: 68 us -> 67.5 us (level)
  no operation moved by 1% of the time
where the time goes in v5:
time: 67.5 us; the launch traced here: 67.3 us
  Pallas kernels  65.7 us (97%)
  local copies, waits for them, and re-layouts  1.67 us (2%)
    pallas_call x1, Pallas kernels, on_device(): pl.pallas_call(functools.partial(kernel, dims), out_shape=jax.ShapeDtypeS...  65.7 us
    unnamed x1, local copies, waits for them, and re-layouts  1.67 us

profile of v5, /device:TPU:13, one launch (start us, length us, event | category | flops | bytes accessed | tf_op | source)
XLA Modules:
  0.0 67.3 jit_solution(11874162839012666121)
XLA Ops:
  0.0 65.7 %shard_map.91 = bf16[128,1024]{1,0:T(8,128)(2,1)} custom-call(bf16[128,1024]{1,0:T(8,128)(2,1)} %bitcast.11, f32[1,1024]{1,0:T(1,128)} %gain_ref.1, f32[1,1024]{1,0:T(1,128)} %bias_ref.1, bf16[128,1024]{1,0:T(8,128)(2,1)} %bitcast.12, s32[4,1,128]{2,1,0:T(1,128)} %bitcast.13, bf16[512,3072]{1,0:T(8,128)(2,1)} %bitcast.7, bf16[512,1024]{1,0:T(8,128)(2,1)} %bitcast.9, ...), custom_call_target="tpu_custom_call" | custom-call | tf_op jit(solution)/shard_map/pallas_call | solution.py:424
  65.7 1.7 %copy.11 = bf16[1,1,128,1024]{3,2,1,0:T(8,128)(2,1)} copy(bf16[1,1,128,1024]{3,2,1,0:T(8,128)(2,1)} %bitcast.8) | data formatting | bytes 524288
